TPU v7x, 32 devices: a whole 2x2x4 slice. The times are simulated.
32 devices in a mesh: sp: 8 (over z, y), ch: 4 (over x, core).
Axes of the slice: x: 2, y: 2, z: 4, core: 2. Of those that a mesh axis runs over, the one named last changes fastest.
Arguments:
- inputs: bfloat16 [8, 37, 37, 256], P('sp', None, None, 'ch'), may hold values from -6 to 6
- cotangent: bfloat16 [8, 19, 19, 728], P('sp', None, None, 'ch'), may hold values from -6 to 6
- kernel_entry: bfloat16 [3, 3, 256], P(None, None, 'ch'), may hold values from -2 to 2
- kernels: bfloat16 [4, 3, 3, 728], P(None, None, None, 'ch'), may hold values from -2 to 2
- project_entry: bfloat16 [2, 728, 256], P(None, 'ch'), may hold values from -0.375 to 0.375
- projects: bfloat16 [4, 728, 728], P(None, 'ch'), may hold values from -0.21875 to 0.21875
- bn_gains: float32 [6, 728], P(None, 'ch'), may hold values from 0.1 to 1.9
- bn_biases: float32 [6, 728], P(None, 'ch'), may hold values from -3 to 3
- run_means: float32 [6, 728], P(None, 'ch'), may hold values from -3 to 3
- run_vars: float32 [6, 728], P(None, 'ch'), may hold values from 0.5 to 2
Outputs:
- output: float32 [8, 19, 19, 728], P('sp', None, None, 'ch')
- grad_inputs: float32 [8, 37, 37, 256], P('sp', None, None, 'ch')
- grad_kernel_entry: float32 [3, 3, 256], P(None, None, 'ch')
- grad_kernels: float32 [4, 3, 3, 728], P(None, None, None, 'ch')
- grad_project_entry: float32 [2, 728, 256], P(None, 'ch')
- grad_projects: float32 [4, 728, 728], P(None, 'ch')
- grad_gains: float32 [6, 728], P(None, 'ch')
- grad_biases: float32 [6, 728], P(None, 'ch')
- new_means: float32 [6, 728], P(None, 'ch')
- new_vars: float32 [6, 728], P(None, 'ch')
All inputs are finite; a program needn't handle non-finite values.
Results may differ from a plain program's by a relative error of at most 0.03.
Values may be sent and summed in bfloat16 or wider, within the bound.
A program may use at most 128 MiB of HBM per device.

v0:
```python
import math
import types

import jax
import jax.numpy as jnp
from jax import lax
from jax.experimental import pallas as pl
from jax.experimental.pallas import tpu as pltpu
from jax.sharding import PartitionSpec as P

MESH = pl.DeviceIdType.MESH
EPSILON = 0.001
MOMENTUM = 0.5
LANE = 128
HALF = 64
F32 = jnp.float32
BF16 = jnp.bfloat16


def round_up(value, step):
    return -(-value // step) * step


UN_S, UN_L, UN_ES, UN_EC, UN_SR, UN_IR, UN_EK, UN_W = 12, 10, 4, 4, 4, 4, 4, 4


def aligned(index, step):
    return index if isinstance(index, int) else pl.multiple_of(index, step)


def repeat(count, one, carry, unroll=4):
    def some(k, carry):
        for j in range(unroll):
            carry = one(k * unroll + j, carry)
        return carry

    whole = count // unroll if count > unroll else 0
    if whole:
        carry = lax.fori_loop(0, whole, some, carry)
    for k in range(whole * unroll, count):
        carry = one(k, carry)
    return carry


def sigmoid(values):
    return 0.5 * jnp.tanh(0.5 * values) + 0.5


def dot(left, right, dims=(1, 0), precision=None):
    return lax.dot_general(
        left,
        right,
        (((dims[0],), (dims[1],)), ((), ())),
        precision=precision,
        preferred_element_type=F32,
    )


def fold(value):
    return jnp.sum(value.reshape(value.shape[0] // 8, 8, value.shape[1]), axis=0)


def geometry(mesh_shape, inputs, cotangent, project_entry, projects):
    geo = types.SimpleNamespace()
    geo.n_sp, geo.n_ch = mesh_shape["sp"], mesh_shape["ch"]
    geo.bands = geo.n_ch // 2
    geo.group = geo.n_sp * geo.bands
    _, geo.hl, geo.wl, geo.ci = inputs.shape
    _, geo.hs, geo.ws, geo.cc = cotangent.shape
    geo.cin, geo.chan = project_entry.shape[2], projects.shape[2]
    geo.wide = round_up(geo.chan, 2 * LANE)
    geo.half = geo.wide // 2
    geo.shard = geo.wide // geo.n_ch
    geo.tiles = geo.half // LANE
    geo.pl_, geo.ps = round_up(geo.wl + 1, 8), round_up(geo.ws + 1, 8)
    geo.bs = 2 * math.ceil(geo.hs / (2 * geo.bands))
    geo.bl = 2 * geo.bs
    geo.rs, geo.rl = geo.bs + 2, geo.bl + 2
    geo.na = 2 * math.ceil(geo.rl / 4)
    geo.nb = geo.rl - geo.na
    geo.ka = geo.na * geo.pl_
    geo.kb = geo.nb * geo.pl_
    geo.full = geo.n_ch * LANE
    geo.ny = geo.bands if geo.n_sp % geo.bands == 0 else 1
    geo.nz = geo.n_sp // geo.ny
    geo.tall = geo.shard // 16
    geo.u_mid = geo.tall * (geo.wide // LANE)
    geo.u_dk = round_up(geo.shard, LANE) // LANE
    geo.u_in = geo.tall * (geo.cin // LANE)
    geo.units = [
        round_up(u, geo.n_sp)
        for u in [geo.u_mid] * 3 + [geo.u_mid // 2] * 2 + [geo.u_in + 4 * geo.u_dk, geo.u_in]
    ]
    geo.plane = geo.bands * geo.ny
    geo.count_large = float(geo.n_sp * geo.hl * geo.wl)
    geo.count_small = float(geo.n_sp * geo.hs * geo.ws)
    return geo


IN_NAMES = [
    "inputs",
    "cotangent",
    "kernel_entry",
    "kernels",
    "project_entry",
    "projects",
    "bn_gains",
    "bn_biases",
    "run_means",
    "run_vars",
]
OUT_NAMES = [
    "m_out",
    "m_gin",
    "m_dke",
    "m_dk",
    "m_dwe",
    "m_dw",
    "m_gains",
    "m_biases",
    "m_means",
    "m_vars",
]


def scratch_table(g):
    dma, vm = pltpu.SemaphoreType.DMA, pltpu.VMEM
    small, large = g.rs * g.ps, g.rl * g.pl_
    cp_rows = (g.bands * g.bl + 2) * g.pl_
    x = g.bands
    table = dict(
        x32=vm((cp_rows, LANE), F32),
        a1=vm((cp_rows + 2 * g.pl_, LANE), F32),
        s1=vm((cp_rows, LANE), F32),
        s1pk=vm((x, g.ka, LANE), BF16),
        s1full=vm((g.ka, g.full), BF16),
        sidepk=vm((x, small, LANE), BF16),
        sidefull=vm((small, g.full), BF16),
        sidecp=vm(((x * g.bs + 2) * g.ps, LANE), F32),
        parloc=vm((56, 2 * LANE), F32),
        parx=vm((x, 56, 2 * LANE), F32),
        par=vm((56, g.half), F32),
        place=vm((g.wide, g.wide), BF16),
        place_in=vm((2, g.cin, g.full), BF16),
        wpad=vm((g.shard, g.wide), BF16),
        w=vm((4, g.half, g.wide), BF16),
        we=vm((2, g.half, g.cin), BF16),
        wp=vm((3, g.half, g.full), BF16),
        cotpad=vm(((x * g.bs + 2) * g.ps, 2 * LANE), F32),
        cotx=vm(((x * g.bs + 2) * g.ps, 2 * LANE), BF16),
        cots=vm((x, small, 2 * LANE), BF16),
        picks=vm((x, 2 * LANE, g.half), F32),
        edge_up=vm((2 * g.pl_, g.half), BF16),
        edge_down=vm((4 * g.pl_, g.half), BF16),
        from_below=vm((2 * g.pl_, g.half), BF16),
        from_above=vm((4 * g.pl_, g.half), BF16),
        cot=vm((small, g.half), F32),
        p1=vm((large, g.half), F32),
        a2=vm((large, g.half), F32),
        s2=vm((g.bl * g.pl_, g.wide), BF16),
        p2=vm((large + 3 * g.pl_, g.half), F32),
        tmp=vm((g.tiles, 48, LANE), F32),
        poolraw=vm((small, g.half), F32),
        pside=vm((small, g.half), F32),
        hid=vm((3, small, g.half), F32),
        act=vm((3, small, g.half), F32),
        sm=vm((3, g.bs * g.ps, g.wide), BF16),
        pm=vm((3, small, g.half), F32),
        gb=vm((3, small, g.half), F32),
        gt=vm((3, small, g.half), F32),
        gs=vm((small, g.half), F32),
        rsend=vm((3, small, g.half), BF16),
        rrecv=vm((3, small, g.half), BF16),
        gside=vm((small, g.half), BF16),
        gt2=vm((large, g.half), F32),
        rsend2=vm((large, g.half), BF16),
        rrecv2=vm((large, g.half), BF16),
        gs2=vm((large, g.half), F32),
        gb1=vm((large, g.half), F32),
        g1=vm((large, g.half), BF16),
        essend=vm((g.ka, x * LANE), BF16),
        esrecv=vm((g.ka, x * LANE), BF16),
        essum=vm((x, g.ka, LANE), BF16),
        esr=vm((x, g.ka, LANE), BF16),
        sdsend=vm((small, x * LANE), BF16),
        sdrecv=vm((small, x * LANE), BF16),
        sdsum=vm((x, small, LANE), BF16),
        sdr=vm((x, small, LANE), BF16),
        gs1=vm((cp_rows, LANE), F32),
        outx=vm((x, g.bs * g.ps, 2 * LANE), BF16),
        outs=vm((x, g.bs * g.ps, 2 * LANE), BF16),
        dk=vm((4, 16, g.half), F32),
        pickb=vm((x, g.half, 2 * LANE), BF16),
        dke=vm((g.n_sp, 16, LANE), F32),
        vec=vm((56, g.half), F32),
        ar2=vm((5, g.group, 2, g.half), F32),
        ar4=vm((4, g.group, 4, g.half), F32),
        ar_ss=dma((9,)),
        ar_rs=dma((9,)),
        s1_ss=dma((2 * g.n_ch,)),
        s1_rs=dma((g.n_ch,)),
        sd_ss=dma((2 * g.n_ch,)),
        sd_rs=dma((g.n_ch,)),
        par_ss=dma((x,)),
        par_rs=dma((x,)),
        we_ss=dma((2, x)),
        we_rs=dma((2, x)),
        w_ss=dma((4, 2 * x)),
        w_rs=dma((4, 2 * x)),
        cot_ss=dma((x,)),
        cot_rs=dma((x,)),
        sm_ss=dma((4,)),
        sm_rs=dma((4,)),
        r_ss=dma((4,)),
        r_rs=dma((4,)),
        halo_ss=dma((7, 2)),
        halo_rs=dma((7, 2)),
        es_ss=dma((2,)),
        es_rs=dma((2,)),
        esx_ss=dma((2, x)),
        esx_rs=dma((2, x)),
        out_ss=dma((x,)),
        out_rs=dma((x,)),
        ra_ss=dma((7, g.plane)),
        ra_rs=dma((7, g.plane)),
        rz_ss=dma((7, g.nz)),
        rz_rs=dma((7, g.nz)),
        gz_ss=dma((5, g.nz)),
        gz_rs=dma((5, g.nz)),
        gy_ss=dma((5, g.ny)),
        gy_rs=dma((5, g.ny)),
        ga_ss=dma((2,)),
        ga_rs=dma((2,)),
        dke_ss=dma((1,)),
        dke_rs=dma((1,)),
    )
    for k, u in enumerate(g.units):
        unit = (16, LANE)
        table.update({
            f"part{k}": vm((x, u) + unit, BF16),
            f"plane{k}": vm((g.plane, u // g.ny) + unit, BF16),
            f"ys{k}": vm((u // g.ny,) + unit, BF16),
            f"rzr{k}": vm((g.nz, u // g.n_sp) + unit, BF16),
            f"fin{k}": vm((u,) + unit, BF16),
        })
    return table


def make_kernel(g, scratch_names):
    n_bands, half, shard, tiles = g.bands, g.half, g.shard, g.tiles
    pitch, pitch_s = g.pl_, g.ps
    small, large = g.rs * g.ps, g.rl * g.pl_
    AVG, VAR, T1, T0, INV, ALPHA, BETA, KAPPA, LAM = (6 * k for k in range(9))
    counts = (g.count_large, g.count_large) + (g.count_small,) * 4

    def kernel(*refs):
        r = types.SimpleNamespace(**dict(zip(IN_NAMES + OUT_NAMES + scratch_names, refs)))
        s = lax.axis_index("sp")
        ch = lax.axis_index("ch")
        x = ch // 2
        c = lax.rem(ch, 2)
        me = s * n_bands + x
        yi, zi = lax.rem(s, g.ny), s // g.ny
        sends = []

        def copy_to(src, dst, send, recv, s_, x_, c_):
            cp = pltpu.make_async_remote_copy(
                src_ref=src,
                dst_ref=dst,
                send_sem=send,
                recv_sem=recv,
                device_id=(s_, x_ * 2 + c_),
                device_id_type=MESH,
            )
            cp.start()
            sends.append(cp.wait_send)

        def landed(ref, sem):
            pltpu.make_async_copy(ref, ref, sem).wait()

        def other_band(k):
            return lax.rem(x + k, n_bands)

        def edge_copy(src_up, dst_up, src_down, dst_down, e):
            up = pltpu.make_async_remote_copy(
                src_up, dst_up, r.halo_ss.at[e, 0], r.halo_rs.at[e, 0],
                device_id=(s, (x - 1) * 2 + c), device_id_type=MESH)
            down = pltpu.make_async_remote_copy(
                src_down, dst_down, r.halo_ss.at[e, 1], r.halo_rs.at[e, 1],
                device_id=(s, (x + 1) * 2 + c), device_id_type=MESH)

            @pl.when(x > 0)
            def _():
                up.start()

            @pl.when(x < n_bands - 1)
            def _():
                down.start()

            def finish():
                @pl.when(x < n_bands - 1)
                def _():
                    landed(dst_up, r.halo_rs.at[e, 0])

                @pl.when(x > 0)
                def _():
                    landed(dst_down, r.halo_rs.at[e, 1])

            def sent():
                @pl.when(x > 0)
                def _():
                    up.wait_send()

                @pl.when(x < n_bands - 1)
                def _():
                    down.wait_send()

            sends.append(sent)
            return finish

        def edges(ref, e):
            first, last = pl.ds(pitch_s, pitch_s), pl.ds(g.bs * pitch_s, pitch_s)
            return edge_copy(
                ref.at[first], ref.at[pl.ds((g.bs + 1) * pitch_s, pitch_s)],
                ref.at[last], ref.at[pl.ds(0, pitch_s)], e)

        def flipped(value, key):
            out, bit = 0, 1
            while bit <= key:
                here = lax.rem(value // bit, 2)
                out = out + bit * (1 - here if key & bit else here)
                bit *= 2
            return out + (value // bit) * bit

        def hops(key):
            return key // (n_bands * g.ny) + key // n_bands % g.ny + key % n_bands

        few = g.group <= 16
        keys = sorted(range(1, g.group), key=hops, reverse=True) if few else []
        peers = [
            (flipped(s, key // n_bands), flipped(x, key % n_bands)) for key in keys
        ]

        def to_group(src, dst, send, recv, pick=None):
            def one(s_, x_):
                pltpu.make_async_remote_copy(
                    src if pick is None else pick(s_, x_), dst, send, recv,
                    device_id=(s_, x_ * 2 + c), device_id_type=MESH).start()

            for s_, x_ in peers:
                one(s_, x_)

            def loop(k, _):
                to = lax.rem(me + k, g.group)
                one(to // n_bands, lax.rem(to, n_bands))
                return 0

            if not few:
                lax.fori_loop(1, g.group, loop, 0)

        sp_keys = sorted(range(1, g.n_sp), key=lambda k: hops(k * n_bands), reverse=True)
        sp_peers = [flipped(s, key) for key in sp_keys] if few else []

        def to_images(src, dst, send, recv):
            def one(s_):
                pltpu.make_async_remote_copy(
                    src, dst, send, recv, device_id=(s_, ch), device_id_type=MESH).start()

            for s_ in sp_peers:
                one(s_)

            def loop(k, _):
                one(lax.rem(s + k, g.n_sp))
                return 0

            if not few:
                lax.fori_loop(1, g.n_sp, loop, 0)

        def sum_start(buf, at, e, rows):
            for k, row in enumerate(rows):
                buf[at, me, k : k + 1, :] = row

            to_group(buf.at[at, me], buf.at[at, me], r.ar_ss.at[e], r.ar_rs.at[e])

        def sum_finish(buf, at, e):
            block = buf.at[at, pl.ds(0, g.group - 1)]
            landed(block, r.ar_rs.at[e])
            sends.append(lambda: landed(block, r.ar_ss.at[e]))
            total = buf[at, 0]
            for k in range(1, g.group):
                total = total + buf[at, k]
            return total

        def fill(ref, start, rows):
            ref[pl.ds(start, rows)] = jnp.zeros((rows,) + ref.shape[1:], ref.dtype)

        def fill_all(ref, step):
            def one(i, _):
                ref[pl.ds(aligned(i * step, 8), step)] = jnp.zeros(
                    (step,) + ref.shape[1:], ref.dtype)
                return 0

            repeat(ref.shape[0] // step, one, 0, 1)

        def lane(t):
            return pl.ds(t * LANE, LANE)

        def col_mask(width, breadth):
            at = lax.broadcasted_iota(jnp.int32, (width, LANE), 0)
            return jnp.where(at < breadth, 1.0, 0.0).astype(F32)

        def row_ok(row, height):
            return jnp.where((row >= 0) & (row < height), 1.0, 0.0).astype(F32)

        mask_l, mask_s = col_mask(pitch, g.wl), col_mask(pitch_s, g.ws)

        def vrow(kind, layer, t):
            return r.vec[kind + layer : kind + layer + 1, lane(t)]

        def taps_of(q, t):
            return [
                [r.par[16 + 4 * (3 * u + v) + q : 17 + 4 * (3 * u + v) + q, lane(t)] for v in range(3)]
                for u in range(3)
            ]

        def flip(taps):
            return [[taps[2 - u][2 - v] for v in range(3)] for u in range(3)]

        def conv_row(rows, taps):
            width = rows[0].shape[0]
            side = [
                rows[0] * taps[0][v] + rows[1] * taps[1][v] + rows[2] * taps[2][v]
                for v in range(3)
            ]
            return side[1] + pltpu.roll(side[0], 1, 0) + pltpu.roll(side[2], width - 1, 0)

        def store_moments(layer, total, square):
            n = counts[layer]
            average = total / n
            variance = square / n - average * average
            inverse = lax.rsqrt(variance + EPSILON)
            alpha = inverse * r.par[layer : layer + 1, :]
            r.vec[AVG + layer : AVG + layer + 1, :] = average
            r.vec[VAR + layer : VAR + layer + 1, :] = variance
            r.vec[INV + layer : INV + layer + 1, :] = inverse
            r.vec[ALPHA + layer : ALPHA + layer + 1, :] = alpha
            r.vec[BETA + layer : BETA + layer + 1, :] = (
                r.par[6 + layer : 7 + layer, :] - average * alpha)

        def store_back(layer, total, product):
            n = counts[layer]
            average = r.vec[AVG + layer : AVG + layer + 1, :]
            inverse = r.vec[INV + layer : INV + layer + 1, :]
            alpha = r.vec[ALPHA + layer : ALPHA + layer + 1, :]
            scaled = inverse * (product - average * total)
            r.vec[T0 + layer : T0 + layer + 1, :] = total
            r.vec[T1 + layer : T1 + layer + 1, :] = scaled
            kappa = -alpha * inverse * scaled / n
            r.vec[KAPPA + layer : KAPPA + layer + 1, :] = kappa
            r.vec[LAM + layer : LAM + layer + 1, :] = -alpha * total / n - kappa * average

        def rowsum(value):
            return jnp.sum(value, axis=0, keepdims=True)

        barrier = pltpu.get_barrier_semaphore()

        def greet(s_, x_):
            pl.semaphore_signal(
                barrier, inc=1, device_id=(s_, x_ * 2 + c), device_id_type=MESH)

        def greet_some(k, _):
            to = lax.rem(me + k, g.group)
            greet(to // n_bands, lax.rem(to, n_bands))
            return 0

        for s_, x_ in peers:
            greet(s_, x_)
        if not few:
            lax.fori_loop(1, g.group, greet_some, 0)
        pl.semaphore_signal(
            barrier, inc=1, device_id=(s, x * 2 + 1 - c), device_id_type=MESH)

        fill_all(r.x32, pitch)
        fill_all(r.a1, pitch)
        fill(r.s1, 0, pitch)
        fill(r.s1, (g.hl + 1) * pitch, (n_bands * g.bl + 1 - g.hl) * pitch)
        fill(r.parloc, 0, 56)
        fill_all(r.wpad, 16)
        fill(r.tmp, 0, tiles)
        fill(r.p2, 0, 3 * pitch)
        fill(r.p2, (g.bl + 3) * pitch, 2 * pitch)
        fill(r.gb1, 0, pitch)
        fill(r.gb1, (g.bl + 1) * pitch, pitch)
        fill(r.dk, 0, 4)
        r.dke[s] = jnp.zeros((16, LANE), F32)
        for first, edge in ((0, x == 0), ((g.bs + 1) * pitch_s, x == n_bands - 1)):
            @pl.when(edge)
            def _():
                for i in range(3):
                    for ref in (r.pm, r.gb):
                        ref[i, first : first + pitch_s] = jnp.zeros((pitch_s, half), F32)

        def entry_silu(row, _):
            value = r.inputs[0, row].astype(F32)
            r.x32[pl.ds(aligned((row + 1) * pitch, 8), g.wl), 0 : g.ci] = value
            r.a1[pl.ds(aligned((row + 2) * pitch, 8), g.wl), 0 : g.ci] = value * sigmoid(value)
            return 0

        repeat(g.hl, entry_silu, 0, UN_ES)
        r.parloc[0:6, 0 : g.cc] = r.bn_gains[...]
        r.parloc[6:12, 0 : g.cc] = r.bn_biases[...]
        for j in range(9):
            at = 16 + 4 * j
            r.parloc[at : at + 4, 0 : g.cc] = r.kernels[j // 3, j % 3].astype(F32)
        taps_in = [
            [r.kernel_entry[u].astype(F32)[v : v + 1, :] for v in range(3)] for u in range(3)
        ]
        pad_in = jnp.zeros((1, LANE - g.ci), F32)
        taps_in = [[jnp.concatenate([k, pad_in], axis=1) for k in row] for row in taps_in]

        def entry_conv(row, _):
            rows = [
                r.a1[pl.ds(aligned((row + 1 + u) * pitch, 8), pitch), :] for u in range(3)
            ]
            r.s1[pl.ds(aligned((row + 1) * pitch, 8), pitch), :] = (
                conv_row(rows, taps_in) * mask_l)
            return 0

        repeat(g.hl, entry_conv, 0, UN_EC)
        for b in range(n_bands):
            for k in range(g.na // 2):
                packed = r.s1[(b * g.bl + 2 * k) * pitch : (b * g.bl + 2 * k + 2) * pitch, :]
                if 2 * k < g.nb:
                    at = (b * g.bl + g.na + 2 * k) * pitch
                    packed = packed + pltpu.roll(r.s1[at : at + 2 * pitch, :], HALF, 1)
                r.s1pk[b, 2 * k * pitch : (2 * k + 2) * pitch, :] = packed.astype(BF16)
        for e in range(2):
            r.wpad[0 : g.cc, 0 : g.cin] = r.project_entry[:, e, :]
            r.we[e, pl.ds(aligned(x * shard, 16), shard), :] = r.wpad[:, 0 : g.cin]

        pl.semaphore_wait(barrier, g.group)
        tile = c * n_bands + x

        def full_lanes(t):
            return pl.ds(aligned(t * LANE, LANE), LANE)

        for k in range(1, n_bands):
            b = other_band(k)
            copy_to(r.s1pk.at[b], r.s1full.at[:, full_lanes(tile)],
                    r.s1_ss.at[k], r.s1_rs.at[tile], s, b, c)
        copy_to(r.s1pk.at[x], r.s1full.at[:, full_lanes(tile)],
                r.s1_ss.at[0], r.s1_rs.at[tile], s, x, 1 - c)
        r.s1full[:, full_lanes(tile)] = r.s1pk[x]
        for k in range(1, n_bands):
            mine = r.we.at[0, pl.ds(aligned(x * shard, 16), shard)]
            copy_to(mine, mine, r.we_ss.at[0, k], r.we_rs.at[0, x], s, other_band(k), c)

        for b in range(n_bands):
            spot = lax.broadcasted_iota(jnp.int32, (2 * LANE, half), 1) - b * shard
            r.picks[b] = jnp.where(
                (spot == lax.broadcasted_iota(jnp.int32, (2 * LANE, half), 0)) & (spot < g.cc),
                1.0, 0.0).astype(F32)
        r.parx[x] = r.parloc[...]

        def send_vectors():
            for k in range(1, n_bands):
                copy_to(r.parx.at[x], r.parx.at[x], r.par_ss.at[k], r.par_rs.at[x],
                        s, other_band(k), c)

        def vectors_landed():
            total = 0.0
            for k in range(1, n_bands):
                b = other_band(k)
                landed(r.parx.at[b], r.par_rs.at[b])
            for b in range(n_bands):
                total = total + dot(r.parx[b], r.picks[b], precision=lax.Precision.HIGHEST)
            r.par[...] = total

        r.sidecp[...] = jnp.zeros_like(r.sidecp)

        def side_row(row, _):
            at = aligned((2 * row + 1) * pitch, 8)
            r.sidecp[pl.ds(aligned((row + 1) * pitch_s, 8), g.ws), :] = r.x32[
                pl.ds(at, g.ws, stride=2), :]
            return 0

        repeat(g.hs, side_row, 0, UN_SR)
        for b in range(n_bands):
            r.sidepk[b] = r.sidecp[b * g.bs * pitch_s : b * g.bs * pitch_s + small, :].astype(BF16)
        r.sidefull[:, full_lanes(tile)] = r.sidepk[x]

        def send_side():
            for k in range(1, n_bands):
                b = other_band(k)
                copy_to(r.sidepk.at[b], r.sidefull.at[:, full_lanes(tile)],
                        r.sd_ss.at[k], r.sd_rs.at[tile], s, b, c)
            copy_to(r.sidepk.at[x], r.sidefull.at[:, full_lanes(tile)],
                    r.sd_ss.at[0], r.sd_rs.at[tile], s, x, 1 - c)
            for k in range(1, n_bands):
                mine = r.we.at[1, pl.ds(aligned(x * shard, 16), shard)]
                copy_to(mine, mine, r.we_ss.at[1, k], r.we_rs.at[1, x], s, other_band(k), c)

        fill_all(r.cotpad, pitch_s)

        def cot_row(row, _):
            r.cotpad[pl.ds(aligned((row + 1) * pitch_s, 8), g.ws), 0 : g.cc] = (
                r.cotangent[0, row].astype(F32))
            return 0

        repeat(g.hs, cot_row, 0, UN_SR)
        r.cotx[...] = r.cotpad[...].astype(BF16)
        r.cots[x] = r.cotx[pl.ds(aligned(x * g.bs * pitch_s, 16), small), :]

        def send_cotangent():
            for k in range(1, n_bands):
                b = other_band(k)
                copy_to(r.cotx.at[pl.ds(aligned(b * g.bs * pitch_s, 16), small)], r.cots.at[x],
                        r.cot_ss.at[k], r.cot_rs.at[x], s, b, c)

        def channel_place(rows, k0, cols, cut, offset):
            k_at = k0 + lax.broadcasted_iota(jnp.int32, (rows, cols), 0)
            p_at = lax.broadcasted_iota(jnp.int32, (rows, cols), 1)
            want = k_at + offset(0)
            for j in range(1, g.n_ch):
                jump = offset(j) - offset(j - 1)
                want = want + jnp.where(k_at >= j * cut, jump, 0)
            return jnp.where(want == p_at, 1.0, 0.0).astype(BF16)

        def offset_wide(j):
            return (j % 2) * half + (j // 2) * shard - j * g.cc

        def offset_in(j):
            return ((j % 2) * n_bands + j // 2) * LANE - j * g.ci

        r.place_in[0] = channel_place(g.cin, 0, g.full, g.ci, offset_in)
        r.place_in[1] = channel_place(
            g.cin, 0, g.full, g.ci, lambda j: offset_in(j) + HALF)
        def place_rows(k, _):
            at = aligned(k * 64, 64)
            r.place[pl.ds(at, 64), :] = channel_place(64, at, g.wide, g.cc, offset_wide)
            return 0

        repeat(g.wide // 64, place_rows, 0, 2)
        fill_all(r.wpad, 16)

        def weight_prepare(q):
            r.wpad[0 : g.cc, 0 : g.chan] = r.projects[:, q, :]
            r.w[q, pl.ds(aligned(x * shard, 16), shard), :] = dot(
                r.wpad[...], r.place[...]).astype(BF16)

        odd = lax.rem(yi, 2) if g.ny > 1 else 0
        pair = zi * g.ny + yi + 1 - 2 * odd
        halves = 2 if g.ny > 1 else 1

        def shard_part(q, b, part):
            size = shard // halves
            return r.w.at[q, pl.ds(aligned(b * shard + part * size, 16), size)]

        def weight_send(q):
            mine = shard_part(q, x, odd)
            for k in range(1, n_bands):
                copy_to(mine, mine, r.w_ss.at[q, k], r.w_rs.at[q, x], s, other_band(k), c)

        def weight_forward(q):
            for k in range(1, n_bands):
                b = other_band(k)
                got = shard_part(q, b, odd)
                landed(got, r.w_rs.at[q, b])
                if halves > 1:
                    copy_to(got, got, r.w_ss.at[q, n_bands + k], r.w_rs.at[q, n_bands + b],
                            pair, x, c)

        def weight_landed(q):
            for k in range(1, n_bands):
                b = other_band(k)
                if halves > 1:
                    landed(shard_part(q, b, 1 - odd), r.w_rs.at[q, n_bands + b])

        weight_prepare(0)
        weight_send(0)
        weight_prepare(1)
        weight_prepare(2)

        for k in range(1, n_bands):
            t = c * n_bands + other_band(k)
            landed(r.s1full.at[:, full_lanes(t)], r.s1_rs.at[t])
            copy_to(r.s1full.at[:, full_lanes(t)], r.s1full.at[:, full_lanes(t)],
                    r.s1_ss.at[g.n_ch + k], r.s1_rs.at[t], s, x, 1 - c)

        for k in range(1, n_bands):
            b = other_band(k)
            landed(r.we.at[0, pl.ds(aligned(b * shard, 16), shard)], r.we_rs.at[0, b])
        for a in range(2):
            r.wp[a] = dot(r.we[0], r.place_in[a]).astype(BF16)

        for k in range(n_bands):
            t = (1 - c) * n_bands + k
            landed(r.s1full.at[:, full_lanes(t)], r.s1_rs.at[t])
        r.p1[0 : g.ka, :] = dot(r.s1full[...], r.wp[0], (1, 1))
        r.p1[g.ka : large, :] = dot(r.s1full[0 : g.kb, :], r.wp[1], (1, 1))

        def moments(ref, first, rows, width):
            out = [[], []]
            for t in range(tiles):
                def one(k, carry):
                    v = ref[pl.ds(aligned((first + k) * width, 8), width), lane(t)]
                    return (carry[0] + fold(v), carry[1] + fold(v * v))

                zero = jnp.zeros((8, LANE), F32)
                total, square = repeat(rows, one, (zero, zero), UN_S if width == pitch_s else UN_L)
                out[0].append(rowsum(total))
                out[1].append(rowsum(square))
            return [jnp.concatenate(o, axis=1) for o in out]

        sum_start(r.ar2, 0, 0, moments(r.p1, 1, g.bl, pitch))
        send_vectors()
        send_side()
        weight_send(1)
        weight_send(2)
        weight_prepare(3)
        weight_forward(0)
        vectors_landed()
        total = sum_finish(r.ar2, 0, 0)
        store_moments(0, total[0:1], total[1:2])

        for t in range(tiles):
            alpha, beta = vrow(ALPHA, 0, t), vrow(BETA, 0, t)

            def one(k, _):
                at = pl.ds(aligned(k * pitch, 8), pitch)
                h = r.p1[at, lane(t)] * alpha + beta
                ok = mask_l * row_ok(x * g.bl + k - 1, g.hl)
                r.a2[at, lane(t)] = h * sigmoid(h) * ok
                return 0

            repeat(g.rl, one, 0, UN_L)
        mine_lanes = aligned(c * half, LANE)
        their_lanes = aligned((1 - c) * half, LANE)

        def own_tile(t):
            return pl.ds(aligned(c * half + t * LANE, LANE), LANE)

        def conv_pairs(source, q, target, row0, rows, height, width, mask):
            for t in range(tiles):
                taps = taps_of(q, t)

                def one(k, _):
                    block = [
                        source[pl.ds(aligned((2 * k + u) * width, 8), width), lane(t)]
                        for u in range(4)
                    ]
                    out = [
                        conv_row(block[j : j + 3], taps) * (mask * row_ok(row0 + 2 * k + j, height))
                        for j in range(2)
                    ]
                    target[pl.ds(aligned(k * 2 * width, 16), 2 * width), own_tile(t)] = (
                        jnp.concatenate(out, axis=0).astype(BF16))
                    return 0

                repeat(rows // 2, one, 0, UN_S if width == pitch_s else UN_L)

        conv_pairs(r.a2, 0, r.s2, x * g.bl, g.bl, g.hl, pitch, mask_l)

        def swap_start(ref, e):
            mine = ref.at[:, pl.ds(mine_lanes, half)]
            copy_to(mine, mine, r.sm_ss.at[e], r.sm_rs.at[e], s, x, 1 - c)

        def swap_landed(ref, e):
            landed(ref.at[:, pl.ds(their_lanes, half)], r.sm_rs.at[e])

        swap_start(r.s2, 0)
        weight_landed(0)
        rows_all = g.bl * pitch
        step = rows_all // 2
        for k in range(2):
            rows = pl.ds(k * step, step)
            r.p2[3 * pitch + k * step : 3 * pitch + (k + 1) * step, :] = dot(
                r.s2[rows, pl.ds(mine_lanes, half)], r.w[0, :, pl.ds(mine_lanes, half)], (1, 1))
        for k in range(1, n_bands):
            t = c * n_bands + other_band(k)
            landed(r.sidefull.at[:, full_lanes(t)], r.sd_rs.at[t])
            copy_to(r.sidefull.at[:, full_lanes(t)], r.sidefull.at[:, full_lanes(t)],
                    r.sd_ss.at[g.n_ch + k], r.sd_rs.at[t], s, x, 1 - c)
        swap_landed(r.s2, 0)
        for k in range(2):
            rows = pl.ds(k * step, step)
            at = slice(3 * pitch + k * step, 3 * pitch + (k + 1) * step)
            r.p2[at, :] = r.p2[at, :] + dot(
                r.s2[rows, pl.ds(their_lanes, half)], r.w[0, :, pl.ds(their_lanes, half)], (1, 1))
        for k in range(1, n_bands):
            b = other_band(k)
            landed(r.we.at[1, pl.ds(aligned(b * shard, 16), shard)], r.we_rs.at[1, b])
        r.wp[2] = dot(r.we[1], r.place_in[0]).astype(BF16)
        for k in range(n_bands):
            t = (1 - c) * n_bands + k
            landed(r.sidefull.at[:, full_lanes(t)], r.sd_rs.at[t])
        r.pside[...] = dot(r.sidefull[...], r.wp[2], (1, 1))
        sum_start(r.ar4, 0, 1,
                  moments(r.p2, 3, g.bl, pitch) + moments(r.pside, 1, g.bs, pitch_s))
        r.edge_up[...] = r.p2[3 * pitch : 5 * pitch, :].astype(BF16)
        r.edge_down[...] = r.p2[(g.bl - 1) * pitch : (g.bl + 3) * pitch, :].astype(BF16)
        edges_done = edge_copy(r.edge_up, r.from_below, r.edge_down, r.from_above, 0)
        weight_send(3)
        weight_forward(1)

        edges_done()

        @pl.when(x > 0)
        def _():
            r.p2[0 : 3 * pitch, :] = r.from_above[...].astype(F32)[pitch : 4 * pitch]

        @pl.when(x < n_bands - 1)
        def _():
            r.p2[(g.bl + 3) * pitch : (g.bl + 5) * pitch, :] = r.from_below[...].astype(F32)

        for t in range(tiles):
            def one(k, _):
                v = (r.p2[pl.ds(aligned(2 * k * pitch, 8), pitch), lane(t)]
                     + r.p2[pl.ds(aligned((2 * k + 1) * pitch, 8), pitch), lane(t)]
                     + r.p2[pl.ds(aligned((2 * k + 2) * pitch, 8), pitch), lane(t)])
                r.tmp[t, 0:pitch, :] = v + pltpu.roll(v, 1, 0) + pltpu.roll(v, pitch - 1, 0)
                r.poolraw[pl.ds(aligned(k * pitch_s, 8), pitch_s), lane(t)] = r.tmp[
                    t, pl.ds(0, pitch_s, stride=2), :]
                return 0

            repeat(g.rs, one, 0, UN_S)
        weight_forward(2)
        total = sum_finish(r.ar4, 0, 1)
        store_moments(1, total[0:1], total[1:2])
        store_moments(2, total[2:3], total[3:4])

        at_col = lax.broadcasted_iota(jnp.int32, (pitch_s, LANE), 0)
        col_count = mask_s * (
            1.0
            + jnp.where(at_col > 0, 1.0, 0.0)
            + jnp.where(2 * at_col + 1 < g.wl, 1.0, 0.0)) * (1.0 / 9.0)

        def window_count(row):
            inside = jnp.where(row > 0, 1.0, 0.0) + jnp.where(2 * row + 1 < g.hl, 1.0, 0.0) + 1.0
            return col_count * (inside.astype(F32) * row_ok(row, g.hs))

        for t in range(tiles):
            alpha, beta = vrow(ALPHA, 1, t) * (1.0 / 9.0), vrow(BETA, 1, t)
            alpha_2, beta_2 = vrow(ALPHA, 2, t), vrow(BETA, 2, t)

            def one(k, _):
                at = pl.ds(aligned(k * pitch_s, 8), pitch_s)
                row = x * g.bs + k - 1
                ok = mask_s * row_ok(row, g.hs)
                h = (r.poolraw[at, lane(t)] * alpha + window_count(row) * beta
                     + r.pside[at, lane(t)] * alpha_2 + beta_2) * ok
                r.hid[0, at, lane(t)] = h
                r.act[0, at, lane(t)] = h * sigmoid(h)
                return 0

            repeat(g.rs, one, 0, UN_S)

        def make_picks():
            for b in range(n_bands):
                spot_b = lax.broadcasted_iota(jnp.int32, (half, 2 * LANE), 0) - b * shard
                r.pickb[b] = jnp.where(
                    (spot_b == lax.broadcasted_iota(jnp.int32, (half, 2 * LANE), 1))
                    & (spot_b < g.cc), 1.0, 0.0).astype(BF16)

        own_rows = slice(pitch_s, (g.bs + 1) * pitch_s)
        for i in range(3):
            if i > 0:
                for t in range(tiles):
                    alpha, beta = vrow(ALPHA, 2 + i, t), vrow(BETA, 2 + i, t)

                    def one(k, _):
                        at = pl.ds(aligned(k * pitch_s, 8), pitch_s)
                        ok = mask_s * row_ok(x * g.bs + k - 1, g.hs)
                        h = (r.pm[i - 1, at, lane(t)] * alpha + beta) * ok
                        r.hid[i, at, lane(t)] = h
                        r.act[i, at, lane(t)] = h * sigmoid(h)
                        return 0

                    repeat(g.rs, one, 0, UN_S)
            conv_pairs(r.act.at[i], i + 1, r.sm.at[i], x * g.bs, g.bs, g.hs,
                       pitch_s, mask_s)
            swap_start(r.sm.at[i], 1 + i)
            weight_landed(1 + i)
            part = dot(r.sm[i, :, pl.ds(mine_lanes, half)],
                       r.w[1 + i, :, pl.ds(mine_lanes, half)], (1, 1))
            swap_landed(r.sm.at[i], 1 + i)
            r.pm[i, own_rows, :] = part + dot(
                r.sm[i, :, pl.ds(their_lanes, half)],
                r.w[1 + i, :, pl.ds(their_lanes, half)], (1, 1))
            if i < 2:
                sum_start(r.ar2, 1 + i, 2 + i, moments(r.pm.at[i], 1, g.bs, pitch_s))
                edges_done = edges(r.pm.at[i], 1 + i)
                if i == 0:
                    send_cotangent()
                    weight_forward(3)
                total = sum_finish(r.ar2, 1 + i, 2 + i)
                store_moments(3 + i, total[0:1], total[1:2])
                edges_done()

        def grad_sums(gref, pref, width, first, rows):
            out = [[], []]
            for t in range(tiles):
                def one(k, carry):
                    at = pl.ds(aligned((first + k) * width, 8), width)
                    v = gref[at, lane(t)]
                    return (carry[0] + fold(v), carry[1] + fold(v * pref[at, lane(t)]))

                zero = jnp.zeros((8, LANE), F32)
                a, b = repeat(rows, one, (zero, zero), UN_S if width == pitch_s else UN_L)
                out[0].append(rowsum(a))
                out[1].append(rowsum(b))
            return [jnp.concatenate(o, axis=1) for o in out]

        for k in range(1, n_bands):
            b = other_band(k)
            landed(r.cots.at[b], r.cot_rs.at[b])
        total = 0.0
        for b in range(n_bands):
            total = total + dot(r.cots[b], r.picks[b].astype(BF16))
        r.cot[...] = total
        sum_start(r.ar4, 1, 4,
                  moments(r.pm.at[2], 1, g.bs, pitch_s)
                  + grad_sums(r.cot, r.pm.at[2], pitch_s, 1, g.bs))
        edges_done = edges(r.pm.at[2], 3)
        make_picks()
        total = sum_finish(r.ar4, 1, 4)
        store_moments(5, total[0:1], total[1:2])
        store_back(5, total[2:3], total[3:4])
        edges_done()

        def norm_back(layer, gref, pref, target, rows, width, mask, row0, height):
            for t in range(tiles):
                alpha, kappa, lam = vrow(ALPHA, layer, t), vrow(KAPPA, layer, t), vrow(LAM, layer, t)

                def one(k, _):
                    at = pl.ds(aligned(k * width, 8), width)
                    ok = mask * row_ok(row0 + k, height)
                    target[at, lane(t)] = (
                        gref[at, lane(t)] * alpha + pref[at, lane(t)] * kappa + lam) * ok
                    return 0

                repeat(rows, one, 0, UN_S if width == pitch_s else UN_L)

        def kernel_grad(aref, gref, q, rows, width):
            for t in range(tiles):
                def one(k, carry):
                    gv = gref[pl.ds(aligned((k + 1) * width, 8), width), lane(t)]
                    turned = [pltpu.roll(gv, width - 1, 0), gv, pltpu.roll(gv, 1, 0)]
                    out = []
                    for u in range(3):
                        av = aref[pl.ds(aligned((k + u) * width, 8), width), lane(t)]
                        for v in range(3):
                            out.append(carry[3 * u + v] + fold(av * turned[v]))
                    return tuple(out)

                zero = jnp.zeros((8, LANE), F32)
                sums = repeat(rows, one, (zero,) * 9, UN_S if width == pitch_s else UN_L)
                for j in range(9):
                    r.dk[q, j : j + 1, lane(t)] = rowsum(sums[j])


        def block_of(name, k):
            return getattr(r, f"{name}{k}")

        def put_units(k, value, first, cols):
            value = value[:, first : first + cols].astype(BF16)
            for b in range(n_bands):
                for t in range(cols // LANE):
                    part = value[b * shard : (b + 1) * shard, t * LANE : (t + 1) * LANE]
                    block_of("part", k)[b, t * g.tall : (t + 1) * g.tall] = (
                        part.reshape(g.tall, 16, LANE))

        def put_kernels():
            for q in range(4):
                value = r.dk[q].astype(BF16)
                for b in range(n_bands):
                    part = dot(value, r.pickb[b]).astype(BF16)
                    for t in range(g.u_dk):
                        at = g.u_in + q * g.u_dk + t
                        r.part5[b, at] = part[:, t * LANE : (t + 1) * LANE]

        def plane_send(k):
            part = g.units[k] // g.ny
            me_plane = x * g.ny + yi
            for key in range(1, g.plane):
                to = lax.rem(me_plane + key, g.plane)
                x_, y_ = to // g.ny, lax.rem(to, g.ny)
                copy_to(block_of("part", k).at[x_, pl.ds(y_ * part, part)],
                        block_of("plane", k).at[me_plane],
                        r.ra_ss.at[k, key], r.ra_rs.at[k, me_plane], zi * g.ny + y_, x_, c)

        def plane_sum_z_send(k):
            part = g.units[k] // g.ny
            me_plane = x * g.ny + yi
            total = block_of("part", k)[x, pl.ds(yi * part, part)].astype(F32)
            for key in range(1, g.plane):
                b = lax.rem(me_plane + key, g.plane)
                landed(block_of("plane", k).at[b], r.ra_rs.at[k, b])
                total = total + block_of("plane", k)[b].astype(F32)
            block_of("ys", k)[...] = total.astype(BF16)
            piece = part // g.nz
            for j in range(1, g.nz):
                to = lax.rem(zi + j, g.nz)
                copy_to(block_of("ys", k).at[pl.ds(to * piece, piece)], block_of("rzr", k).at[zi],
                        r.rz_ss.at[k, j], r.rz_rs.at[k, zi], to * g.ny + yi, x, c)

        def z_sum(k):
            part = g.units[k] // g.ny
            piece = part // g.nz
            total = block_of("ys", k)[pl.ds(zi * piece, piece)].astype(F32)
            for j in range(1, g.nz):
                b = lax.rem(zi + j, g.nz)
                landed(block_of("rzr", k).at[b], r.rz_rs.at[k, b])
                total = total + block_of("rzr", k)[b].astype(F32)
            at = pl.ds(yi * part + zi * piece, piece)
            block_of("fin", k)[at] = total.astype(BF16)
            return at

        def z_gather(k):
            at = z_sum(k)
            for j in range(1, g.nz):
                to = lax.rem(zi + j, g.nz)
                copy_to(block_of("fin", k).at[at], block_of("fin", k).at[at],
                        r.gz_ss.at[k, j], r.gz_rs.at[k, zi], to * g.ny + yi, x, c)

        def all_gather(k):
            mine = block_of("fin", k).at[z_sum(k)]
            to_images(mine, mine, r.ga_ss.at[k - 5], r.ga_rs.at[k - 5])

        def y_gather(k):
            part = g.units[k] // g.ny
            piece = part // g.nz
            for j in range(1, g.nz):
                b = lax.rem(zi + j, g.nz)
                landed(block_of("fin", k).at[pl.ds(yi * part + b * piece, piece)],
                       r.gz_rs.at[k, b])
            at = pl.ds(yi * part, part)
            for j in range(1, g.ny):
                to = lax.rem(yi + j, g.ny)
                copy_to(block_of("fin", k).at[at], block_of("fin", k).at[at],
                        r.gy_ss.at[k, j], r.gy_rs.at[k, yi], zi * g.ny + to, x, c)

        def get_units(k, cols):
            tiles_in = [
                block_of("fin", k)[t * g.tall : (t + 1) * g.tall].reshape(shard, LANE)
                for t in range(cols // LANE)
            ]
            return jnp.concatenate(tiles_in, axis=1)

        def y_landed(k):
            part = g.units[k] // g.ny
            for j in range(1, g.ny):
                b = lax.rem(yi + j, g.ny)
                landed(block_of("fin", k).at[pl.ds(b * part, part)], r.gy_rs.at[k, b])

        def finish_block(k):
            y_landed(k)
            value = dot(get_units(k, g.wide), r.place[...], (1, 1))
            r.m_dw[:, 3 - k, :] = value[0 : g.cc, 0 : g.chan]

        def finish_halves():
            y_landed(3)
            y_landed(4)
            value = jnp.concatenate(
                [get_units(3, g.wide // 2), get_units(4, g.wide // 2)], axis=1)
            value = dot(value, r.place[...], (1, 1))
            r.m_dw[:, 0, :] = value[0 : g.cc, 0 : g.chan]

        def finish_entry(k):
            piece = g.units[k] // g.n_sp
            others = block_of("fin", k).at[pl.ds(0, (g.n_sp - 1) * piece)]
            landed(others, r.ga_rs.at[k - 5])
            sends.append(lambda: landed(others, r.ga_ss.at[k - 5]))
            r.m_dwe[:, 6 - k, :] = get_units(k, g.cin).astype(F32)[0 : g.cc]
            if k == 5:
                for q in range(4):
                    at = g.u_in + q * g.u_dk
                    value = jnp.concatenate(
                        [r.fin5[at + t] for t in range(g.u_dk)], axis=1).astype(F32)
                    for j in range(9):
                        r.m_dk[j // 3, j % 3, q : q + 1, :] = value[j : j + 1, 0 : g.cc]

        def output_landed():
            for k in range(1, n_bands):
                b = other_band(k)
                landed(r.outs.at[b], r.out_rs.at[b])
            for b in range(n_bands):
                value = r.outs[b].astype(F32)
                for k in range(g.bs):
                    if b * g.bs + k < g.hs:
                        r.m_out[b * g.bs + k, :, 0, :] = value[
                            k * pitch_s : k * pitch_s + g.ws, 0 : g.cc]

        def send_output():
            for k in range(1, n_bands):
                b = other_band(k)
                copy_to(r.outx.at[b], r.outs.at[x], r.out_ss.at[k], r.out_rs.at[x], s, b, c)

        for i in (2, 1, 0):
            layer = 3 + i
            gref = r.cot if i == 2 else r.gb.at[i + 1]
            norm_back(layer, gref, r.pm.at[i], r.gt.at[i], g.rs, pitch_s, mask_s,
                      x * g.bs - 1, g.hs)
            grad = r.gt[i].astype(BF16)
            r.rsend[i] = dot(grad, r.w[1 + i, :, pl.ds(their_lanes, half)]).astype(BF16)
            copy_to(r.rsend.at[i], r.rrecv.at[i], r.r_ss.at[i], r.r_rs.at[i], s, x, 1 - c)
            part = dot(grad, r.w[1 + i, :, pl.ds(mine_lanes, half)])
            grad = r.gt[i, own_rows, :].astype(BF16)
            put_units(2 - i, dot(grad, r.sm[i], (0, 0)), 0, g.wide)
            landed(r.rrecv.at[i], r.r_rs.at[i])
            r.gs[...] = part + r.rrecv[i].astype(F32)
            rows = [[] for _ in range(4 if i == 0 else 2)]
            for t in range(tiles):
                taps = flip(taps_of(i + 1, t))

                def one(k, carry):
                    block = [
                        r.gs[pl.ds(aligned((k + u) * pitch_s, 8), pitch_s), lane(t)]
                        for u in range(3)
                    ]
                    at = pl.ds(aligned((k + 1) * pitch_s, 8), pitch_s)
                    row = x * g.bs + k
                    h = r.hid[i, at, lane(t)]
                    sig = sigmoid(h)
                    value = conv_row(block, taps) * (sig * (1.0 + h * (1.0 - sig))) * (
                        mask_s * row_ok(row, g.hs))
                    if i == 0:
                        value = value + r.cot[at, lane(t)]
                    r.gb[i, at, lane(t)] = value
                    if i == 0:
                        new = [
                            value, value * r.pside[at, lane(t)],
                            value * window_count(row),
                            value * r.poolraw[at, lane(t)] * (1.0 / 9.0)]
                    else:
                        new = [value, value * r.pm[i - 1, at, lane(t)]]
                    return tuple(a + fold(b) for a, b in zip(carry, new))

                zero = jnp.zeros((8, LANE), F32)
                sums = repeat(g.bs, one, (zero,) * len(rows), UN_S)
                for j, v in enumerate(sums):
                    rows[j].append(rowsum(v))
            rows = [jnp.concatenate(o, axis=1) for o in rows]
            buf, at_e, e = ((r.ar4, 2, 7), (r.ar2, 3, 6), (r.ar2, 4, 5))[i]
            sum_start(buf, at_e, e, rows)
            edges_done = edges(r.gb.at[i], 4 + i)
            plane_send(2 - i)
            if i < 2:
                plane_sum_z_send(1 - i)
            if i == 0:
                z_gather(0)
            kernel_grad(r.act.at[i], r.gs, i + 1, g.bs, pitch_s)
            if i == 2:
                value = []
                for t in range(tiles):
                    h = (r.pm[2, own_rows, lane(t)] * vrow(ALPHA, 5, t) + vrow(BETA, 5, t)
                         + r.hid[0, own_rows, lane(t)])
                    value.append(h.astype(BF16))
                value = jnp.concatenate(value, axis=1)
                for b in range(n_bands):
                    r.outx[b] = dot(value, r.pickb[b]).astype(BF16)
                r.outs[x] = r.outx[x]
            total = sum_finish(buf, at_e, e)
            if i > 0:
                store_back(layer - 1, total[0:1], total[1:2])
            else:
                store_back(2, total[0:1], total[1:2])
                store_back(1, total[2:3], total[3:4])
            edges_done()

        for t in range(tiles):
            alpha, kappa, lam = vrow(ALPHA, 1, t) * (1.0 / 9.0), vrow(KAPPA, 1, t), vrow(LAM, 1, t)

            def spread(v):
                r.tmp[t, pl.ds(0, pitch_s, stride=2), :] = v
                r.tmp[t, pl.ds(1, pitch_s, stride=2), :] = v + pltpu.roll(v, pitch_s - 1, 0)
                return r.tmp[t, 0:pitch, :]

            def one(k, _):
                low = r.gb[0, pl.ds(aligned(k * pitch_s, 8), pitch_s), lane(t)]
                high = r.gb[0, pl.ds(aligned((k + 1) * pitch_s, 8), pitch_s), lane(t)]
                for j, v in enumerate((low + high, high)):
                    row = x * g.bl + 2 * k + j - 1
                    ok = mask_l * row_ok(row, g.hl)
                    p = r.p2[pl.ds(aligned((2 * k + j + 2) * pitch, 8), pitch), lane(t)]
                    r.gt2[pl.ds(aligned((2 * k + j) * pitch, 8), pitch), lane(t)] = (
                        spread(v) * alpha + p * kappa + lam) * ok
                return 0

            repeat(g.bs + 1, one, 0, UN_S)
        for k in range(2):
            at = pl.ds(k * (large // 2), large // 2)
            r.rsend2[at, :] = dot(
                r.gt2[at, :].astype(BF16), r.w[0, :, pl.ds(their_lanes, half)]).astype(BF16)
        copy_to(r.rsend2, r.rrecv2, r.r_ss.at[3], r.r_rs.at[3], s, x, 1 - c)
        for k in range(2):
            at = pl.ds(k * (large // 2), large // 2)
            r.gs2[at, :] = dot(r.gt2[at, :].astype(BF16), r.w[0, :, pl.ds(mine_lanes, half)])
        grad = r.gt2[pitch : (g.bl + 1) * pitch, :].astype(BF16)
        hw = g.wide // 2
        put_units(3, dot(grad, r.s2[:, 0:hw], (0, 0)), 0, hw)
        plane_send(3)
        put_units(4, dot(grad, r.s2[:, hw:], (0, 0)), 0, hw)
        z_gather(1)
        y_gather(0)
        landed(r.rrecv2, r.r_rs.at[3])
        r.gs2[...] = r.gs2[...] + r.rrecv2[...].astype(F32)
        rows = [[], []]
        for t in range(tiles):
            taps = flip(taps_of(0, t))
            alpha, beta = vrow(ALPHA, 0, t), vrow(BETA, 0, t)

            def one(k, carry):
                block = [
                    r.gs2[pl.ds(aligned((k + u) * pitch, 8), pitch), lane(t)] for u in range(3)
                ]
                at = pl.ds(aligned((k + 1) * pitch, 8), pitch)
                p = r.p1[at, lane(t)]
                h = p * alpha + beta
                sig = sigmoid(h)
                value = conv_row(block, taps) * (sig * (1.0 + h * (1.0 - sig))) * (
                    mask_l * row_ok(x * g.bl + k, g.hl))
                r.gb1[at, lane(t)] = value
                return (carry[0] + fold(value), carry[1] + fold(value * p))

            zero = jnp.zeros((8, LANE), F32)
            sums = repeat(g.bl, one, (zero, zero), UN_L)
            for j, v in enumerate(sums):
                rows[j].append(rowsum(v))
        rows = [jnp.concatenate(o, axis=1) for o in rows]
        sum_start(r.ar4, 3, 8, rows)
        plane_send(4)
        plane_sum_z_send(2)

        def own_ok(k, width_rows):
            return jnp.where((k >= 1) & (k <= width_rows), 1.0, 0.0).astype(F32)

        for t in range(tiles):
            alpha, kappa, lam = vrow(ALPHA, 2, t), vrow(KAPPA, 2, t), vrow(LAM, 2, t)

            def one(k, _):
                out = []
                for j in range(2):
                    at = pl.ds(aligned((2 * k + j) * pitch_s, 8), pitch_s)
                    ok = mask_s * (row_ok(x * g.bs + 2 * k + j - 1, g.hs) * own_ok(2 * k + j, g.bs))
                    out.append((r.gb[0, at, lane(t)] * alpha
                                + r.pside[at, lane(t)] * kappa + lam) * ok)
                r.gside[pl.ds(aligned(2 * k * pitch_s, 16), 2 * pitch_s), lane(t)] = (
                    jnp.concatenate(out, axis=0).astype(BF16))
                return 0

            repeat(g.rs // 2, one, 0, UN_S)
        own_tiles = pl.ds(aligned(c * n_bands * LANE, LANE), n_bands * LANE)
        their_tiles = pl.ds(aligned((1 - c) * n_bands * LANE, LANE), n_bands * LANE)
        r.sdsend[...] = dot(r.gside[...], r.wp[2, :, their_tiles]).astype(BF16)
        copy_to(r.sdsend, r.sdrecv, r.es_ss.at[1], r.es_rs.at[1], s, x, 1 - c)
        part = dot(r.gside[...], r.wp[2, :, own_tiles])
        landed(r.sdrecv, r.es_rs.at[1])
        part = part + r.sdrecv[...].astype(F32)
        for b in range(n_bands):
            r.sdsum[b] = part[:, b * LANE : (b + 1) * LANE].astype(BF16)
        for k in range(1, n_bands):
            b = other_band(k)
            copy_to(r.sdsum.at[b], r.sdr.at[x], r.esx_ss.at[1, k], r.esx_rs.at[1, x], s, b, c)
        r.sdr[x] = r.sdsum[x]

        lane_at = lax.broadcasted_iota(jnp.int32, (half, g.full), 1)
        low_lanes = lax.rem(lane_at, LANE) < HALF
        both_place = r.place_in[0] + r.place_in[1]

        value = dot(r.gside[...], r.sidefull[...], (0, 0)).astype(BF16)
        put_units(5, dot(value, both_place, (1, 1)), 0, g.cin)
        kernel_grad(r.a2, r.gs2, 0, g.bl, pitch)
        put_kernels()
        plane_send(5)
        y_gather(1)
        plane_sum_z_send(3)
        total = sum_finish(r.ar4, 3, 8)
        store_back(0, total[0:1], total[1:2])

        for t in range(tiles):
            alpha, kappa, lam = vrow(ALPHA, 0, t), vrow(KAPPA, 0, t), vrow(LAM, 0, t)

            def one(k, _):
                out = []
                for j in range(2):
                    at = pl.ds(aligned((2 * k + j) * pitch, 8), pitch)
                    ok = mask_l * (row_ok(x * g.bl + 2 * k + j - 1, g.hl) * own_ok(2 * k + j, g.bl))
                    out.append((r.gb1[at, lane(t)] * alpha + r.p1[at, lane(t)] * kappa + lam) * ok)
                r.g1[pl.ds(aligned(2 * k * pitch, 16), 2 * pitch), lane(t)] = (
                    jnp.concatenate(out, axis=0).astype(BF16))
                return 0

            repeat(g.rl // 2, one, 0, UN_L)

        def entry_part(lanes):
            a = dot(r.g1[0 : g.ka, :], r.wp[0, :, lanes])
            b = dot(r.g1[g.ka : large, :], r.wp[1, :, lanes])
            if g.kb == g.ka:
                return a + b
            return jnp.concatenate([a[0 : g.kb] + b, a[g.kb :]], axis=0)

        r.essend[...] = entry_part(their_tiles).astype(BF16)
        copy_to(r.essend, r.esrecv, r.es_ss.at[0], r.es_rs.at[0], s, x, 1 - c)
        part = entry_part(own_tiles)
        grad_a = dot(r.g1[0 : g.ka, :], r.s1full[...], (0, 0))
        grad_b = dot(r.g1[g.ka : large, :], r.s1full[0 : g.kb, :], (0, 0))
        value = jnp.where(low_lanes, grad_a, grad_b).astype(BF16)
        put_units(6, dot(value, both_place, (1, 1)), 0, g.cin)
        landed(r.esrecv, r.es_rs.at[0])
        part = part + r.esrecv[...].astype(F32)
        for b in range(n_bands):
            r.essum[b] = part[:, b * LANE : (b + 1) * LANE].astype(BF16)
        for k in range(1, n_bands):
            b = other_band(k)
            copy_to(r.essum.at[b], r.esr.at[x], r.esx_ss.at[0, k], r.esx_rs.at[0, x], s, b, c)
        r.esr[x] = r.essum[x]
        plane_send(6)
        z_gather(2)
        plane_sum_z_send(4)
        z_gather(3)
        plane_sum_z_send(5)
        send_output()
        finish_block(0)
        finish_block(1)

        spot = lax.broadcasted_iota(jnp.int32, (half, 2 * LANE), 0) - x * shard
        pick_own = jnp.where(
            (spot == lax.broadcasted_iota(jnp.int32, (half, 2 * LANE), 1)) & (spot < g.cc),
            1.0, 0.0).astype(F32)
        final = dot(r.vec[0:24, :], pick_own, precision=lax.Precision.HIGHEST)
        final = final[:, 0 : g.cc]
        at_row = lax.broadcasted_iota(jnp.int32, (6, g.cc), 0)
        count = jnp.where(at_row < 2, g.count_large, g.count_small)
        bessel = count / (count - 1.0)
        r.m_means[...] = (1.0 - MOMENTUM) * r.run_means[...] + MOMENTUM * final[0:6]
        r.m_vars[...] = (1.0 - MOMENTUM) * r.run_vars[...] + MOMENTUM * (final[6:12] * bessel)
        r.m_gains[...] = final[12:18]
        r.m_biases[...] = final[18:24]

        for k in range(1, n_bands):
            b = other_band(k)
            landed(r.sdr.at[b], r.esx_rs.at[1, b])
        for b in range(n_bands):
            r.sidecp[b * g.bs * pitch_s : (b + 1) * g.bs * pitch_s, :] = (
                r.sdr[b].astype(F32)[pitch_s : (g.bs + 1) * pitch_s])
        for k in range(1, n_bands):
            b = other_band(k)
            landed(r.esr.at[b], r.esx_rs.at[0, b])
        fill(r.gs1, 0, pitch)
        fill(r.gs1, (n_bands * g.bl + 1) * pitch, pitch)
        for b in range(n_bands):
            for k in range(g.na // 2):
                value = r.esr[b, 2 * k * pitch : (2 * k + 2) * pitch, :].astype(F32)
                for j in range(2):
                    i = 2 * k + j
                    if 1 <= i <= g.bl:
                        at = (b * g.bl + i) * pitch
                        r.gs1[at : at + pitch, :] = value[j * pitch : (j + 1) * pitch]
                if 2 * k < g.nb:
                    value = pltpu.roll(value, HALF, 1)
                    for j in range(2):
                        i = g.na + 2 * k + j
                        if 1 <= i <= g.bl:
                            at = (b * g.bl + i) * pitch
                            r.gs1[at : at + pitch, :] = value[j * pitch : (j + 1) * pitch]
        def entry_kernel(k, carry):
            gv = r.gs1[pl.ds(aligned((k + 1) * pitch, 8), pitch), :]
            turned = [pltpu.roll(gv, pitch - 1, 0), gv, pltpu.roll(gv, 1, 0)]
            out = []
            for u in range(3):
                av = r.a1[pl.ds(aligned((k + 1 + u) * pitch, 8), pitch), :]
                for v in range(3):
                    out.append(carry[3 * u + v] + fold(av * turned[v]))
            return tuple(out)

        zero = jnp.zeros((8, LANE), F32)
        sums = repeat(g.hl, entry_kernel, (zero,) * 9, UN_EK)
        for j in range(9):
            r.dke[s, j : j + 1, :] = rowsum(sums[j])

        to_images(r.dke.at[s], r.dke.at[s], r.dke_ss.at[0], r.dke_rs.at[0])

        taps = flip(taps_in)

        def in_grad(row):
            block = [r.gs1[pl.ds(aligned((row + u) * pitch, 8), pitch), :] for u in range(3)]
            h = r.x32[pl.ds(aligned((row + 1) * pitch, 8), pitch), :]
            sig = sigmoid(h)
            return conv_row(block, taps) * (sig * (1.0 + h * (1.0 - sig)))

        r.tmp[0] = jnp.zeros((48, LANE), F32)

        def in_rows(k, _):
            r.tmp[0, pl.ds(0, pitch_s, stride=2), :] = r.sidecp[
                pl.ds(aligned(k * pitch_s, 8), pitch_s), :]
            value = in_grad(2 * k) + r.tmp[0, 0:pitch, :]
            r.m_gin[2 * k, :, 0, :] = value[0 : g.wl, 0 : g.ci]
            return 0

        def in_odd_rows(k, _):
            r.m_gin[2 * k + 1, :, 0, :] = in_grad(2 * k + 1)[0 : g.wl, 0 : g.ci]
            return 0

        repeat(g.hs, in_rows, 0, UN_IR)
        repeat(g.hl // 2, in_odd_rows, 0, UN_IR)

        y_gather(2)
        plane_sum_z_send(6)
        z_gather(4)
        y_gather(3)
        all_gather(5)
        finish_block(2)
        all_gather(6)
        y_gather(4)
        output_landed()
        finish_entry(5)
        finish_halves()
        finish_entry(6)

        block = r.dke.at[pl.ds(0, g.n_sp - 1)]
        landed(block, r.dke_rs.at[0])
        sends.append(lambda: landed(block, r.dke_ss.at[0]))
        total = r.dke[0]
        for k in range(1, g.n_sp):
            total = total + r.dke[k]
        for u in range(3):
            r.m_dke[u] = total[3 * u : 3 * u + 3, 0 : g.ci]
        for wait in sends:
            wait()

    return kernel


def body(mesh_shape, *args):
    inputs, cotangent, kernel_entry, kernels, project_entry, projects = args[:6]
    g = geometry(mesh_shape, inputs, cotangent, project_entry, projects)
    operands = list(args)
    operands[3] = jnp.transpose(kernels, (1, 2, 0, 3))
    operands[4] = jnp.transpose(project_entry, (1, 0, 2))
    operands[5] = jnp.transpose(projects, (1, 0, 2))
    operands = [pltpu.with_memory_space_constraint(o, pltpu.HBM) for o in operands]
    table = scratch_table(g)
    names = list(table)
    results = [
        (g.hs, g.ws, 1, g.cc),
        (g.hl, g.wl, 1, g.ci),
        kernel_entry.shape,
        operands[3].shape,
        operands[4].shape,
        operands[5].shape,
    ] + [(6, g.cc)] * 4
    results = [jax.ShapeDtypeStruct(shape, F32) for shape in results]
    vmem = pl.BlockSpec(memory_space=pltpu.VMEM)
    parts = pl.pallas_call(
        make_kernel(g, names),
        out_shape=[pltpu.VMEM(o.shape, o.dtype) for o in results],
        in_specs=[vmem] * 10,
        out_specs=[vmem] * 10,
        scratch_shapes=list(table.values()),
        compiler_params=pltpu.CompilerParams(
            collective_id=0, has_side_effects=True, vmem_limit_bytes=54 << 20),
    )(*operands)

    def write(*refs):
        copies = [
            pltpu.make_async_copy(refs[k], refs[10 + k], refs[20].at[k]) for k in range(10)
        ]
        for copy in copies:
            copy.start()
        for copy in copies:
            copy.wait()

    out = pl.pallas_call(
        write,
        out_shape=results,
        in_specs=[vmem] * 10,
        out_specs=[pl.BlockSpec(memory_space=pl.ANY)] * 10,
        scratch_shapes=[pltpu.SemaphoreType.DMA((10,))],
        compiler_params=pltpu.CompilerParams(vmem_limit_bytes=16 << 20),
    )(*parts)
    out = list(out)
    out[0] = jnp.transpose(out[0], (2, 0, 1, 3))
    out[1] = jnp.transpose(out[1], (2, 0, 1, 3))
    out[3] = jnp.transpose(out[3], (2, 0, 1, 3))
    out[4] = jnp.transpose(out[4], (1, 0, 2))
    out[5] = jnp.transpose(out[5], (1, 0, 2))
    return tuple(out)


def solution(mesh):
    mesh_shape = dict(mesh.shape)
    wide = P("sp", None, None, "ch")
    row = P(None, "ch")
    mid = P(None, "ch", None)
    return jax.shard_map(
        lambda *args: body(mesh_shape, *args),
        mesh=mesh,
        in_specs=(wide, wide, P(None, None, "ch"), P(None, None, None, "ch"), mid, mid,
                  row, row, row, row),
        out_specs=(wide, wide, P(None, None, "ch"), P(None, None, None, "ch"), mid, mid,
                   row, row, row, row),
        check_vma=False,
    )
```

profile of v0, /device:TPU:0, one launch (start us, length us, event | category | flops | bytes accessed | tf_op | source)
XLA Modules:
  0.0 118.1 jit_solution(10426475013520444591)
XLA Ops:
  0.6 115.3 %shard_map.177 = (f32[19,19,1,182]{3,2,1,0:T(1,128)S(1)}, f32[37,37,1,64]{3,2,1,0:T(1,128)S(1)}, f32[3,3,64]{2,1,0:T(4,128)S(1)}, f32[3,3,4,182]{3,2,1,0:T(4,128...) custom-call(bf16[1,37,37,64]{3,2,1,0:T(8,128)(2,1)} %refs_0_.1, ...), custom_call_target="tpu_custom_call" | custom-call | tf_op jit(solution)/shard_map/pallas_call | solution.py:1455
  116.0 2.0 %shard_map.178 = (f32[19,19,1,182]{3,2,1,0:T(1,128)}, f32[37,37,1,64]{3,2,1,0:T(1,128)}, f32[3,3,64]{2,1,0:T(4,128)}, f32[3,3,4,182]{3,2,1,0:T(4,128)}, f32[182,...) custom-call(f32[19,19,1,182]{3,2,1,0:T(1,128)S(1)} %get-tuple-elemen, ...), custom_call_target="tpu_custom_call" | custom-call | tf_op jit(solution)/shard_map/pallas_call | solution.py:1474
where the time goes:
time: 118 us
  Pallas kernels  117 us (99%)
    pallas_call x1, Pallas kernels, body(): pl.pallas_call(make_kernel(g, names), out_shape=[pltpu.VMEM(o.shape, o.dt...  115 us

commit v1 on v0

--- a/solution.py
+++ b/solution.py
@@ -193,8 +193,8 @@
         pickb=vm((x, g.half, 2 * LANE), BF16),
         dke=vm((g.n_sp, 16, LANE), F32),
         vec=vm((56, g.half), F32),
-        ar2=vm((5, g.group, 2, g.half), F32),
-        ar4=vm((4, g.group, 4, g.half), F32),
+        ar2=vm((6, g.group, 2, g.half), F32),
+        ar4=vm((3, g.group, 4, g.half), F32),
         ar_ss=dma((9,)),
         ar_rs=dma((9,)),
         s1_ss=dma((2 * g.n_ch,)),
@@ -262,6 +262,14 @@
         me = s * n_bands + x
         yi, zi = lax.rem(s, g.ny), s // g.ny
         sends = []
+        older = [0]
+
+        def drain():
+            for wait in sends[: older[0]]:
+                wait()
+            del sends[: older[0]]
+            older[0] = 0
+
 
         def copy_to(src, dst, send, recv, s_, x_, c_):
             cp = pltpu.make_async_remote_copy(
@@ -377,12 +385,14 @@
                 lax.fori_loop(1, g.n_sp, loop, 0)
 
         def sum_start(buf, at, e, rows):
+            older[0] = len(sends)
             for k, row in enumerate(rows):
                 buf[at, me, k : k + 1, :] = row
 
             to_group(buf.at[at, me], buf.at[at, me], r.ar_ss.at[e], r.ar_rs.at[e])
 
         def sum_finish(buf, at, e):
+            drain()
             block = buf.at[at, pl.ds(0, g.group - 1)]
             landed(block, r.ar_rs.at[e])
             sends.append(lambda: landed(block, r.ar_ss.at[e]))
@@ -717,8 +727,8 @@
         send_side()
         weight_send(1)
         weight_send(2)
+        weight_forward(0)
         weight_prepare(3)
-        weight_forward(0)
         vectors_landed()
         total = sum_finish(r.ar2, 0, 0)
         store_moments(0, total[0:1], total[1:2])
@@ -1228,9 +1238,9 @@
             for j, v in enumerate(sums):
                 rows[j].append(rowsum(v))
         rows = [jnp.concatenate(o, axis=1) for o in rows]
-        sum_start(r.ar4, 3, 8, rows)
+        sum_start(r.ar2, 5, 8, rows)
+        plane_sum_z_send(2)
         plane_send(4)
-        plane_sum_z_send(2)
 
         def own_ok(k, width_rows):
             return jnp.where((k >= 1) & (k <= width_rows), 1.0, 0.0).astype(F32)
@@ -1275,7 +1285,7 @@
         plane_send(5)
         y_gather(1)
         plane_sum_z_send(3)
-        total = sum_finish(r.ar4, 3, 8)
+        total = sum_finish(r.ar2, 5, 8)
         store_back(0, total[0:1], total[1:2])
 
         for t in range(tiles):
@@ -1315,6 +1325,7 @@
             b = other_band(k)
             copy_to(r.essum.at[b], r.esr.at[x], r.esx_ss.at[0, k], r.esx_rs.at[0, x], s, b, c)
         r.esr[x] = r.essum[x]
+        older[0] = len(sends)
         plane_send(6)
         z_gather(2)
         plane_sum_z_send(4)
@@ -1344,6 +1355,7 @@
         for b in range(n_bands):
             r.sidecp[b * g.bs * pitch_s : (b + 1) * g.bs * pitch_s, :] = (
                 r.sdr[b].astype(F32)[pitch_s : (g.bs + 1) * pitch_s])
+        drain()
         for k in range(1, n_bands):
             b = other_band(k)
             landed(r.esr.at[b], r.esx_rs.at[0, b])

time: 118 us -> 118 us (level)
  no operation moved by 1% of the time
where the time goes in v1:
time: 118 us
  Pallas kernels  117 us (99%)
    pallas_call x1, Pallas kernels, body(): pl.pallas_call(make_kernel(g, names), out_shape=[pltpu.VMEM(o.shape, o.dt...  115 us

profile of v1, /device:TPU:0, one launch (start us, length us, event | category | flops | bytes accessed | tf_op | source)
XLA Modules:
  0.0 117.6 jit_solution(14184405579438400973)
XLA Ops:
  0.6 114.8 %shard_map.177 = (f32[19,19,1,182]{3,2,1,0:T(1,128)S(1)}, f32[37,37,1,64]{3,2,1,0:T(1,128)S(1)}, f32[3,3,64]{2,1,0:T(4,128)S(1)}, f32[3,3,4,182]{3,2,1,0:T(4,128...) custom-call(bf16[1,37,37,64]{3,2,1,0:T(8,128)(2,1)} %refs_0_.1, ...), custom_call_target="tpu_custom_call" | custom-call | tf_op jit(solution)/shard_map/pallas_call | solution.py:1467
  115.4 2.0 %shard_map.178 = (f32[19,19,1,182]{3,2,1,0:T(1,128)}, f32[37,37,1,64]{3,2,1,0:T(1,128)}, f32[3,3,64]{2,1,0:T(4,128)}, f32[3,3,4,182]{3,2,1,0:T(4,128)}, f32[182,...) custom-call(f32[19,19,1,182]{3,2,1,0:T(1,128)S(1)} %get-tuple-elemen, ...), custom_call_target="tpu_custom_call" | custom-call | tf_op jit(solution)/shard_map/pallas_call | solution.py:1486
